TPU v7x, 512 devices: a whole 4x8x8 slice. The times are simulated.
512 devices in a mesh: dp: 16 (over y, core), tensor: 32 (over z, x).
Axes of the slice: x: 4, y: 8, z: 8, core: 2. Of those that a mesh axis runs over, the one named last changes fastest.
Arguments:
- tokens: bfloat16 [2048, 4096], P('dp', 'tensor'), may hold values from -6 to 6
- gate_pre: bfloat16 [2048, 16384], P('dp', 'tensor'), may hold values from -6 to 6
- up_blocks: bfloat16 [32, 64, 128, 128], P('tensor'), may hold values from -0.125 to 0.125
- up_mask: int32 [32, 128], P(None, 'tensor'), may hold values from 0 to 1, as said below
- down_blocks: bfloat16 [32, 64, 128, 128], P('tensor'), may hold values from -0.0625 to 0.0625
- down_mask: int32 [128, 32], replicated, may hold values from 0 to 1, as said below
- down_owner: int32 [128], replicated, may hold values from 0 to 31, as said below
- cotangent: bfloat16 [2048, 4096], P('dp', 'tensor'), may hold values from -6 to 6
Outputs:
- mixed: bfloat16 [2048, 4096], P('dp', 'tensor')
- input_grad: bfloat16 [2048, 4096], P('dp', 'tensor')
- gate_grad: bfloat16 [2048, 16384], P('dp', 'tensor')
- up_grad: bfloat16 [32, 64, 128, 128], P('tensor', 'dp')
- down_grad: bfloat16 [32, 64, 128, 128], P('tensor', 'dp')
Inputs may be any that keep to these rules, and one draw needn't show every extreme that they name: `up_mask`: each column strip of 4 block columns holds exactly 64 ones. `down_mask`: the rows owned by one device hold exactly 64 ones together. `down_owner`: every device owns exactly 4 block rows.
All inputs are finite; a program needn't handle non-finite values.
Results may differ from a plain program's by a relative error of at most 0.022.
Values may be sent and summed in bfloat16 or wider, within the bound.
No kernel may reach another device: no remote copies, remote signals or barrier semaphores. Data moves between devices by JAX's collectives and lax.ppermute only.
A program may use at most 128 MiB of HBM per device.

v0:
```python
import jax
import jax.numpy as jnp
from jax import lax
from jax.sharding import PartitionSpec as P


def kept_positions(marked, total):
    marked = marked.reshape(-1).astype(jnp.int32)
    running = jnp.cumsum(marked) - 1
    target = jnp.where(marked > 0, running, total)
    indices = jnp.arange(marked.shape[0], dtype=jnp.int32)
    return jnp.zeros((total,), jnp.int32).at[target].set(indices, mode="drop")


def one_hot(indices, total):
    return (indices[:, None] == jnp.arange(total, dtype=jnp.int32)[None, :]).astype(jnp.float32)


def row_slots(down_owner, devices):
    marks = (down_owner[:, None] == jnp.arange(devices, dtype=jnp.int32)[None, :]).astype(jnp.int32)
    earlier = jnp.cumsum(marks, axis=0) - marks
    return jnp.sum(earlier * marks, axis=1)


def picker(wanted, block, current, segment):
    block_count = segment.shape[1] // block
    inside = (wanted >= 0) & (wanted < block_count)
    shaped = segment.reshape(segment.shape[0], block_count, block)
    chosen = jnp.take(shaped, jnp.clip(wanted, 0, block_count - 1), axis=1)
    return jnp.where(inside[None, :, None], chosen, current)


def shards(tokens, gate_pre, up_blocks, up_mask, down_blocks, down_mask, down_owner, cotangent):
    devices = lax.axis_size("tensor")
    position = lax.axis_index("tensor")
    token_count = tokens.shape[0]
    blocks_wide = up_mask.shape[0]
    strip_size = up_mask.shape[1]
    block = up_blocks.shape[2]
    kept_up = up_blocks.shape[1]
    kept_down = down_blocks.shape[1]
    model_width = blocks_wide * block
    highest = lax.Precision.HIGHEST
    x_full, dy_full = (
        lax.all_gather(tokens, "tensor", axis=1, tiled=True),
        lax.all_gather(cotangent, "tensor", axis=1, tiled=True),
    )
    token_blocks = x_full.reshape(token_count, blocks_wide, block)
    cot_blocks = dy_full.reshape(token_count, blocks_wide, block)
    w_up = up_blocks[0]
    w_down = down_blocks[0]
    up_pos = kept_positions(up_mask, kept_up)
    up_rows = up_pos // strip_size
    up_cols = up_pos % strip_size
    token_chosen = jnp.take(token_blocks, up_rows, axis=1)
    product = jnp.einsum("nkb,kbc->nkc", token_chosen, w_up, preferred_element_type=jnp.float32)
    up_val = jnp.einsum("nkc,ks->nsc", product, one_hot(up_cols, strip_size), precision=highest)
    gate_val = gate_pre.reshape(token_count, strip_size, block).astype(jnp.float32)
    sigmoid_gate = jax.nn.sigmoid(gate_val)
    activated = gate_val * sigmoid_gate
    hidden = (activated * up_val).astype(jnp.bfloat16).reshape(token_count, strip_size * block)
    my_rows = kept_positions(down_owner == position, strip_size)
    owned_mask = jnp.take(down_mask, my_rows, axis=0)
    down_pos = kept_positions(owned_mask, kept_down)
    slots = down_pos // blocks_wide
    down_cols = down_pos % blocks_wide
    empty = jnp.zeros((token_count, strip_size, block), jnp.bfloat16)
    hidden_owned = picker(
        my_rows, block, empty, lax.all_gather(hidden, "tensor", axis=1, tiled=True)
    )
    h_chosen = jnp.take(hidden_owned, slots, axis=1)
    product = jnp.einsum("nkb,kbc->nkc", h_chosen, w_down, preferred_element_type=jnp.float32)
    out_part = jnp.einsum(
        "nkc,kj->njc", product, one_hot(down_cols, blocks_wide), precision=highest
    )
    out_part = out_part.astype(jnp.bfloat16).reshape(1, token_count, model_width)
    dy_chosen = jnp.take(cot_blocks, down_cols, axis=1)
    down_term = jnp.einsum("nkb,nkc->kbc", h_chosen, dy_chosen, preferred_element_type=jnp.float32)[
        None
    ]
    backward = jnp.einsum("nkc,kbc->nkb", dy_chosen, w_down, preferred_element_type=jnp.float32)
    dh_owned = jnp.einsum("nkb,ka->nab", backward, one_hot(slots, strip_size), precision=highest)
    dh_owned = dh_owned.astype(jnp.bfloat16).reshape(token_count, strip_size * block)
    home_index = down_owner * strip_size + row_slots(down_owner, devices)
    targets = position * strip_size + jnp.arange(strip_size, dtype=jnp.int32)
    wanted = jnp.take(home_index, targets)
    hidden_grad = picker(
        wanted, block, empty, lax.all_gather(dh_owned, "tensor", axis=1, tiled=True)
    )
    dh_float = hidden_grad.astype(jnp.float32)
    gate_grad = (dh_float * up_val * sigmoid_gate * (1.0 + gate_val * (1.0 - sigmoid_gate))).astype(
        jnp.bfloat16
    )
    gate_grad = gate_grad.reshape(token_count, strip_size * block)
    up_act_grad = (dh_float * activated).astype(jnp.bfloat16)
    du_chosen = jnp.take(up_act_grad, up_cols, axis=1)
    product = jnp.einsum("nkc,kbc->nkb", du_chosen, w_up, preferred_element_type=jnp.float32)
    in_part = jnp.einsum("nkb,kr->nrb", product, one_hot(up_rows, blocks_wide), precision=highest)
    in_part = in_part.astype(jnp.bfloat16).reshape(1, token_count, model_width)
    up_term = jnp.einsum(
        "nkb,nkc->kbc", token_chosen, du_chosen, preferred_element_type=jnp.float32
    )[None]
    out_pieces, in_pieces = (
        lax.all_to_all(out_part, "tensor", split_axis=2, concat_axis=0, tiled=True),
        lax.all_to_all(in_part, "tensor", split_axis=2, concat_axis=0, tiled=True),
    )
    mixed = jnp.sum(out_pieces.astype(jnp.float32), axis=0).astype(jnp.bfloat16)
    input_grad = jnp.sum(in_pieces.astype(jnp.float32), axis=0).astype(jnp.bfloat16)
    up_sum, down_sum = (
        lax.psum_scatter(
            up_term.astype(jnp.bfloat16), "dp", scatter_dimension=1, tiled=True
        ).astype(jnp.float32),
        lax.psum_scatter(
            down_term.astype(jnp.bfloat16), "dp", scatter_dimension=1, tiled=True
        ).astype(jnp.float32),
    )
    up_grad = up_sum.astype(jnp.bfloat16)
    down_grad = down_sum.astype(jnp.bfloat16)
    return (mixed, input_grad, gate_grad, up_grad, down_grad)


def solution(mesh):
    placed = (
        P("dp", "tensor"),
        P("dp", "tensor"),
        P("tensor", None, None, None),
        P(None, "tensor"),
        P("tensor", None, None, None),
        P(),
        P(),
        P("dp", "tensor"),
    )
    return jax.shard_map(
        shards,
        mesh=mesh,
        in_specs=placed,
        out_specs=(
            P("dp", "tensor"),
            P("dp", "tensor"),
            P("dp", "tensor"),
            P("tensor", "dp", None, None),
            P("tensor", "dp", None, None),
        ),
        check_vma=False,
    )
```

profile of v0, /device:TPU:2, one launch (start us, length us, event | category | flops | bytes accessed | tf_op | source)
XLA Modules:
  0.0 517.0 jit_solution(11576796951660111175)
XLA Ops:
  18.4 79.6 %all-gather.9.cloned.1.call-done = bf16[128,4096]{0,1:T(8,128)(2,1)} async-done(((bf16[128,128]{0,1:T(8,128)(2,1)}), bf16[128,4096]{0,1:T(8,128)(2,1)}) %all-gather.9.cloned.1.call-update) | async-done | bytes 1048592 | tf_op jit(solution)/shard_map/all_gather | solution.py:46
  99.6 2.2 gather_fusion.5
  101.8 3.8 convolution_bitcast_fusion.1
  105.7 3.8 fusion.48
  115.2 66.1 %all-gather.5.cloned.1.call-done = bf16[128,4096]{0,1:T(8,128)(2,1)} async-done(((bf16[128,128]{0,1:T(8,128)(2,1)}), bf16[128,4096]{0,1:T(8,128)(2,1)}) %all-gather.5.cloned.1.call-update) | async-done | bytes 1048592 | tf_op jit(solution)/shard_map/all_gather | solution.py:45
  182.9 2.2 gather_fusion.2
  185.0 4.3 convolution_bitcast_fusion.3
  189.4 80.9 %all-gather.11.cloned.1.call-done = bf16[128,16384]{0,1:T(8,128)(2,1)} async-done(((bf16[128,512]{0,1:T(8,128)(2,1)}), bf16[128,16384]{0,1:T(8,128)(2,1)}) %all-gather.11.cloned.1.call-update) | async-done | bytes 4194320 | tf_op jit(solution)/shard_map/all_gather | solution.py:88
  270.3 6.4 %copy.134 = bf16[128,128,128]{2,0,1:T(8,128)(2,1)} copy(bf16[128,128,128]{0,2,1:T(8,128)(2,1)} %bitcast.106) | data formatting | bytes 8388608 | tf_op jit(solution)/shard_map/reshape | solution.py:28
  276.7 2.8 gather_fusion.6
  279.4 6.0 %fusion.54 = (bf16[128,4,128]{2,1,0:T(4,128)(2,1)S(1)}, bf16[128,4,128]{2,1,0:T(4,128)(2,1)S(1)}, bf16[128,4,128]{2,1,0:T(4,128)(2,1)S(1)}) fusion(f32[128,4,128]{2,1,0:T(4,128)S(1)} %reshape.234, bf16[4,128,128]{2,1,0:T(8,128)(2,1)S(1)} %gather_fusion.6, pred[4]{0:T(512)(128)(4,1)S(1)} %copy-done.17, pred[4]{0:T(512)(128)(4,1)S(1)} %copy-done.16, ...), kind=kOutput, calls=%fused_computation.55 | convolution fusion | flops 51511552 | bytes 4981000 | tf_op jit(solution)/shard_map/nkc,ks->nsc/dot_general | solution.py:57
  286.4 2.2 gather_fusion.7
  288.6 4.6 convert_bitcast_fusion.1
  293.9 5.2 %convolution_bitcast_fusion = f32[128,64,128]{2,0,1:T(8,128)} fusion(bf16[1,64,128,128]{3,2,1,0:T(8,128)(2,1)S(1)} %copy-done, bf16[64,128,128]{2,1,0:T(8,128)(2,1)} %gather_fusion.7, pred[64]{0:T(512)(128)(4,1)S(1)} %copy-done.6), kind=kOutput, calls=%fused_computation.19 | convolution fusion | flops 269484032 | bytes 8388672 | tf_op jit(solution)/shard_map/nkc,kbc->nkb/dot_general | solution.py:97
  299.1 72.1 %all-gather.7.cloned.1.call-done = bf16[128,16384]{0,1:T(8,128)(2,1)} async-done(((bf16[128,512]{0,1:T(8,128)(2,1)}), bf16[128,16384]{0,1:T(8,128)(2,1)}) %all-gather.7.cloned.1.call-update) | async-done | bytes 4194320 | tf_op jit(solution)/shard_map/all_gather | solution.py:69
  371.2 6.5 %copy.125 = bf16[128,128,128]{2,0,1:T(8,128)(2,1)} copy(bf16[128,128,128]{0,2,1:T(8,128)(2,1)} %bitcast.107) | data formatting | bytes 8388608 | tf_op jit(solution)/shard_map/reshape | solution.py:28
  377.7 2.8 gather_fusion.3
  380.6 2.1 gather_fusion.4
  382.8 4.6 convert_bitcast_fusion
  387.9 6.1 %fusion.36 = bf16[128,32,128]{2,1,0:T(8,128)(2,1)S(1)} fusion(f32[128,64,128]{2,0,1:T(8,128)} %convolution_bitcast_fusion, s32[64]{0:T(128)S(1)} %copy-done.14), kind=kOutput, calls=%fused_computation.45 | convolution fusion | flops 403179520 | bytes 5243136 | tf_op jit(solution)/shard_map/nkb,kr->nrb/dot_general | solution.py:98
  394.5 2.8 copy.138
  397.9 22.4 %reduce.15 = bf16[4096,128]{1,0:T(8,128)(2,1)S(1)} reduce(bf16[4096,1,128]{2,1,0:T(2,128)(2,1)S(1)} %bitcast.102, bf16[]{:T(256)} %broadcast.484), dimensions={1}, to_apply=%bitcast.95.reduce_sub_computation | reduce | bytes 2097154
  421.4 7.0 %all-to-all-start.1 = ((bf16[32,2,8192]{2,1,0:T(2,128)(2,1)}), bf16[32,2,8192]{2,1,0:T(2,128)(2,1)S(1)}, u32[]{:S(2)}, u32[]{:S(2)}) async-start(bf16[32,2,8192]{2,1,0:T(2,128)(2,1)} %reshape.359), calls=%async_computation.1 | async-start | bytes 2097152 | tf_op jit(solution)/shard_map/all_to_all | solution.py:105
  428.4 2.4 convolution_bitcast_fusion.2
  430.8 4.1 fusion.39
  436.2 5.0 copy.129
  441.2 23.4 %reduce.14 = bf16[4096,128]{1,0:T(8,128)(2,1)} reduce(bf16[4096,1,128]{2,1,0:T(2,128)(2,1)S(1)} %bitcast.103, bf16[]{:T(256)} %broadcast.484), dimensions={1}, to_apply=%bitcast.93.reduce_sub_computation | reduce | bytes 2097154
  464.6 2.1 reshape.357
  466.7 9.8 %all-to-all-start = ((bf16[32,2,8192]{2,1,0:T(2,128)(2,1)}), bf16[32,2,8192]{2,1,0:T(2,128)(2,1)}, u32[]{:S(2)}, u32[]{:S(2)}) async-start(bf16[32,2,8192]{2,1,0:T(2,128)(2,1)} %reshape.357), calls=%async_computation | async-start | bytes 2097152 | tf_op jit(solution)/shard_map/all_to_all | solution.py:104
  479.3 22.0 %all-to-all-done = bf16[32,2,8192]{2,1,0:T(2,128)(2,1)} async-done(((bf16[32,2,8192]{2,1,0:T(2,128)(2,1)}), bf16[32,2,8192]{2,1,0:T(2,128)(2,1)}, u32[]{:S(2)}, u32[]{:S(2)}) %all-to-all-start) | async-done | bytes 1048608 | tf_op jit(solution)/shard_map/all_to_all | solution.py:104
  501.3 5.8 %reshape.358 = bf16[4096,1,128]{2,1,0:T(2,128)(2,1)} reshape(bf16[32,2,8192]{2,1,0:T(2,128)(2,1)} %all-to-all-done) | data formatting | bytes 2097152
  507.1 1.9 copy.147
  (116 shorter events, 29.3 us)
Async XLA Ops:
  7.2 177.9 %copy-start = (bf16[1,64,128,128]{3,2,1,0:T(8,128)(2,1)S(1)}, bf16[1,64,128,128]{3,2,1,0:T(8,128)(2,1)}, u32[]{:S(2)}) copy-start(bf16[1,64,128,128]{3,2,1,0:T(8,128)(2,1)} %param.16) | copy-start | bytes 6291460
  7.2 90.8 %all-gather.9.cloned.1.call-start = ((), (), s32[]{:S(2)}) async-start(), calls=%async_computation.6 | async-start | bytes 1081344 | tf_op jit(solution)/shard_map/all_gather | solution.py:46
  8.9 172.4 %all-gather.5.cloned.1.call-start = ((), (), s32[]{:S(2)}) async-start(), calls=%async_computation.4 | async-start | bytes 1081344 | tf_op jit(solution)/shard_map/all_gather | solution.py:45
  10.4 259.9 %all-gather.11.cloned.1.call-start = ((), (), s32[]{:S(2)}) async-start(), calls=%async_computation.7 | async-start | bytes 4325376 | tf_op jit(solution)/shard_map/all_gather | solution.py:88
  18.3 83.5 %copy-start.11 = (s32[64]{0:T(128)}, s32[64]{0:T(128)S(1)}, u32[]{:S(2)}) copy-start(s32[64]{0:T(128)S(1)} %get-tuple-element.20) | copy-start | bytes 772
  18.3 87.3 %copy-start.4 = (s32[64]{0:T(128)}, s32[64]{0:T(128)S(1)}, u32[]{:S(2)}) copy-start(s32[64]{0:T(128)S(1)} %get-tuple-element.33) | copy-start | bytes 772
  105.6 4.7 copy-start.9
  105.7 5.0 copy-start.3
  110.3 260.9 %all-gather.7.cloned.1.call-start = ((), (), s32[]{:S(2)}) async-start(), calls=%async_computation.5 | async-start | bytes 4325376 | tf_op jit(solution)/shard_map/all_gather | solution.py:69
  114.6 0.5 copy-start.13
  114.6 70.4 %copy-start.7 = (pred[64]{0:T(512)(128)(4,1)}, pred[64]{0:T(512)(128)(4,1)S(1)}, u32[]{:S(2)}) copy-start(pred[64]{0:T(512)(128)(4,1)S(1)} %get-tuple-element.38) | copy-start | bytes 196
  270.3 9.2 %copy-start.15 = (s32[64]{0:T(128)S(1)}, s32[64]{0:T(128)}, u32[]{:S(2)}) copy-start(s32[64]{0:T(128)} %get-tuple-element.14) | copy-start | bytes 772
  270.3 9.2 %copy-start.16 = (pred[4]{0:T(512)(128)(4,1)S(1)}, pred[4]{0:T(512)(128)(4,1)}, u32[]{:S(2)}) copy-start(pred[4]{0:T(512)(128)(4,1)} %get-tuple-element.15) | copy-start | bytes 16
  270.3 9.2 %copy-start.17 = (pred[4]{0:T(512)(128)(4,1)S(1)}, pred[4]{0:T(512)(128)(4,1)}, u32[]{:S(2)}) copy-start(pred[4]{0:T(512)(128)(4,1)} %get-tuple-element.17) | copy-start | bytes 16
  286.3 223.6 %reduce-scatter.3.cloned.1.call-start = ((), (), s32[]{:S(2)}) async-start(), calls=%async_computation.8 | async-start | bytes 2228224 | tf_op jit(solution)/shard_map/reduce_scatter | solution.py:110
  286.4 2.2 copy-start.6
  286.4 2.2 copy-start.8
  293.2 0.7 copy-start.10
  293.2 0.7 copy-start.5
  293.2 216.7 %reduce-scatter.5.cloned.1.call-start = ((), (), s32[]{:S(2)}) async-start(), calls=%async_computation.9 | async-start | bytes 2228224 | tf_op jit(solution)/shard_map/reduce_scatter | solution.py:113
  387.3 0.6 copy-start.14
  420.2 8.2 %copy-start.2 = (bf16[64,128,128]{2,1,0:T(8,128)(2,1)S(1)}, bf16[64,128,128]{2,1,0:T(8,128)(2,1)}, u32[]{:S(2)}) copy-start(bf16[64,128,128]{2,1,0:T(8,128)(2,1)} %gather_fusion.4) | copy-start | bytes 6291460
  421.4 45.4 %all-to-all-start.1 = ((bf16[32,2,8192]{2,1,0:T(2,128)(2,1)}), bf16[32,2,8192]{2,1,0:T(2,128)(2,1)S(1)}, u32[]{:S(2)}, u32[]{:S(2)}) async-start(bf16[32,2,8192]{2,1,0:T(2,128)(2,1)} %reshape.359), calls=%async_computation.1 | async-start | bytes 2097152 | tf_op jit(solution)/shard_map/all_to_all | solution.py:105
  428.4 2.4 copy-start.12
  466.7 34.6 %all-to-all-start = ((bf16[32,2,8192]{2,1,0:T(2,128)(2,1)}), bf16[32,2,8192]{2,1,0:T(2,128)(2,1)}, u32[]{:S(2)}, u32[]{:S(2)}) async-start(bf16[32,2,8192]{2,1,0:T(2,128)(2,1)} %reshape.357), calls=%async_computation | async-start | bytes 2097152 | tf_op jit(solution)/shard_map/all_to_all | solution.py:104
  507.1 2.8 copy-start.1
Sparse Core Ops, SparseCore 0:
  11.8 86.1 all-gather.8
  101.7 79.5 all-gather.4
  185.0 85.2 all-gather.10
  286.4 84.7 all-gather.6
  374.4 59.0 reduce-scatter.2
  436.8 61.4 reduce-scatter.4
where the time goes:
time: 525 us; the launch traced here: 517 us
  waiting for transfers between devices  321 us (61%)
  local copies, waits for them, and re-layouts  67 us (13%)
  other arithmetic  52.4 us (10%)
  matrix products  44.8 us (9%)
  starting transfers between devices  17.1 us (3%)
  between operations  14.8 us (3%)
    all_gather x1, waiting for transfers between devices, shards(): lax.all_gather(dh_owned, 'tensor', axis=1, tiled=True)  80.9 us
    all_gather x1, waiting for transfers between devices, shards(): lax.all_gather(cotangent, 'tensor', axis=1, tiled=True)  79.6 us
    all_gather x1, waiting for transfers between devices, shards(): lax.all_gather(hidden, 'tensor', axis=1, tiled=True)  72.1 us
    all_gather x1, waiting for transfers between devices, shards(): lax.all_gather(tokens, 'tensor', axis=1, tiled=True)  66.1 us
    unnamed x2, other arithmetic  45.8 us
    all_to_all x1, waiting for transfers between devices, shards(): lax.all_to_all(out_part, 'tensor', split_axis=2, concat_axis=0, tiled=True)  22 us
    unnamed x50, local copies, waits for them, and re-layouts  20.5 us
    reshape x2, local copies, waits for them, and re-layouts, picker(): shaped = segment.reshape(segment.shape[0], block_count, block)  12.9 us
  transfers between devices with their start and end apart: 8, of which 5 were waited for; matrix products, arithmetic and copies ran while one was open for 28% of the time, Pallas kernels for 0%

commit v1 on v0

--- a/solution.py
+++ b/solution.py
@@ -43,7 +43,9 @@
     highest = lax.Precision.HIGHEST
     x_full, dy_full = (
         lax.all_gather(tokens, "tensor", axis=1, tiled=True),
-        lax.all_gather(cotangent, "tensor", axis=1, tiled=True),
+        jnp.concatenate(
+            lax.all_to_all(jnp.stack([cotangent] * lax.axis_size("tensor")), "tensor", 0, 0), axis=1
+        ),
     )
     token_blocks = x_full.reshape(token_count, blocks_wide, block)
     cot_blocks = dy_full.reshape(token_count, blocks_wide, block)

time: 525 us -> 442 us (0.84)
  waiting for transfers between devices: 321 us -> 229 us
  starting transfers between devices: 17.1 us -> 30.5 us
    all_gather x1 -> x0, waiting for transfers between devices: 79.6 us -> none  [shards(): lax.all_gather(cotangent, 'tensor', axis=1, tiled=True)]
    all_gather x1, waiting for transfers between devices: 66.1 us -> 30.4 us  [shards(): lax.all_gather(tokens, 'tensor', axis=1, tiled=True)]
    all_to_all x0 -> x1, waiting for transfers between devices: none -> 23.7 us  [shards(): lax.all_to_all(jnp.stack([cotangent] * lax.axis_size('tensor')), 'tensor'...]
    all_to_all x0 -> x1, starting transfers between devices: none -> 13.5 us  [shards(): lax.all_to_all(jnp.stack([cotangent] * lax.axis_size('tensor')), 'tensor'...]
    unnamed x50 -> x53, local copies, waits for them, and re-layouts: 20.5 us -> 18.7 us
  transfers between devices with their start and end apart: 8 -> 8, of which waited for: 5 -> 5; matrix products, arithmetic and copies ran while one was open for 28% -> 32% of each run, Pallas kernels for 0% -> 0%
where the time goes in v1:
time: 442 us; the launch traced here: 435 us
  waiting for transfers between devices  229 us (52%)
  local copies, waits for them, and re-layouts  65.6 us (15%)
  other arithmetic  49.8 us (11%)
  matrix products  44.8 us (10%)
  starting transfers between devices  30.5 us (7%)
  between operations  14.5 us (3%)
    all_gather x1, waiting for transfers between devices, shards(): lax.all_gather(dh_owned, 'tensor', axis=1, tiled=True)  80.9 us
    all_gather x1, waiting for transfers between devices, shards(): lax.all_gather(hidden, 'tensor', axis=1, tiled=True)  72.2 us
    unnamed x2, other arithmetic  45.8 us
    all_gather x1, waiting for transfers between devices, shards(): lax.all_gather(tokens, 'tensor', axis=1, tiled=True)  30.4 us
    all_to_all x1, waiting for transfers between devices, shards(): lax.all_to_all(jnp.stack([cotangent] * lax.axis_size('tensor')), 'tensor'...  23.7 us
    all_to_all x1, waiting for transfers between devices, shards(): lax.all_to_all(out_part, 'tensor', split_axis=2, concat_axis=0, tiled=True)  22 us
    unnamed x53, local copies, waits for them, and re-layouts  18.7 us
    all_to_all x1, starting transfers between devices, shards(): lax.all_to_all(jnp.stack([cotangent] * lax.axis_size('tensor')), 'tensor'...  13.5 us
  transfers between devices with their start and end apart: 8, of which 5 were waited for; matrix products, arithmetic and copies ran while one was open for 32% of the time, Pallas kernels for 0%

profile of v1, /device:TPU:2, one launch (start us, length us, event | category | flops | bytes accessed | tf_op | source)
XLA Modules:
  0.0 434.5 jit_solution(12245935906272836593)
XLA Ops:
  10.9 13.5 %all-to-all-start.1 = ((bf16[32,128,128]{2,1,0:T(8,128)(2,1)}), bf16[32,128,128]{2,1,0:T(8,128)(2,1)S(1)}, u32[]{:S(2)}, u32[]{:S(2)}) async-start(bf16[32,128,128]{2,1,0:T(8,128)(2,1)} %stack.2), calls=%async_computation.1 | async-start | bytes 2097152 | tf_op jit(solution)/shard_map/all_to_all | solution.py:47
  29.5 23.7 %all-to-all-done.1 = bf16[32,128,128]{2,1,0:T(8,128)(2,1)S(1)} async-done(((bf16[32,128,128]{2,1,0:T(8,128)(2,1)}), bf16[32,128,128]{2,1,0:T(8,128)(2,1)S(1)}, u32[]{:S(2)}, u32[]{:S(2)}) %all-to-all-start.1) | async-done | bytes 1048608 | tf_op jit(solution)/shard_map/all_to_all | solution.py:47
  53.2 2.2 gather_fusion.5
  55.3 3.8 convolution_bitcast_fusion.1
  59.2 3.8 fusion.48
  68.7 30.4 %all-gather.4.cloned.1.call-done = bf16[128,4096]{0,1:T(8,128)(2,1)} async-done(((bf16[128,128]{0,1:T(8,128)(2,1)}), bf16[128,4096]{0,1:T(8,128)(2,1)}) %all-gather.4.cloned.1.call-update) | async-done | bytes 1048592 | tf_op jit(solution)/shard_map/all_gather | solution.py:45
  100.7 2.2 gather_fusion.2
  102.9 4.3 convolution_bitcast_fusion.3
  107.2 80.9 %all-gather.8.cloned.1.call-done = bf16[128,16384]{0,1:T(8,128)(2,1)} async-done(((bf16[128,512]{0,1:T(8,128)(2,1)}), bf16[128,16384]{0,1:T(8,128)(2,1)}) %all-gather.8.cloned.1.call-update) | async-done | bytes 4194320 | tf_op jit(solution)/shard_map/all_gather | solution.py:90
  188.1 6.4 %copy.126 = bf16[128,128,128]{2,0,1:T(8,128)(2,1)} copy(bf16[128,128,128]{0,2,1:T(8,128)(2,1)} %bitcast.110) | data formatting | bytes 8388608 | tf_op jit(solution)/shard_map/reshape | solution.py:28
  194.5 2.8 gather_fusion.6
  197.3 6.0 %fusion.54 = (bf16[128,4,128]{2,1,0:T(4,128)(2,1)S(1)}, bf16[128,4,128]{2,1,0:T(4,128)(2,1)S(1)}, bf16[128,4,128]{2,1,0:T(4,128)(2,1)S(1)}) fusion(f32[128,4,128]{2,1,0:T(4,128)S(1)} %reshape.236, bf16[4,128,128]{2,1,0:T(8,128)(2,1)S(1)} %gather_fusion.6, pred[4]{0:T(512)(128)(4,1)S(1)} %copy-done.19, pred[4]{0:T(512)(128)(4,1)S(1)} %copy-done.18, ...), kind=kOutput, calls=%fused_computation.55 | convolution fusion | flops 51511552 | bytes 4981000 | tf_op jit(solution)/shard_map/nkc,ks->nsc/dot_general | solution.py:59
  204.3 2.2 gather_fusion.7
  206.5 4.6 %convert_bitcast_fusion.1 = bf16[1,64,128,128]{3,2,1,0:T(8,128)(2,1)} fusion(bf16[64,128,128]{2,1,0:T(8,128)(2,1)} %gather_fusion.2, pred[64]{0:T(512)(128)(4,1)S(1)} %copy-done.10, bf16[64,128,128]{2,1,0:T(8,128)(2,1)} %gather_fusion.7, pred[64]{0:T(512)(128)(4,1)S(1)} %copy-done.8), kind=kOutput, calls=%fused_computation.38 | convolution fusion | flops 271581184 | bytes 6291584 | tf_op jit(solution)/shard_map/nkb,nkc->kbc/dot_general | solution.py:102
  211.7 5.2 %convolution_bitcast_fusion = f32[128,64,128]{2,0,1:T(8,128)} fusion(bf16[1,64,128,128]{3,2,1,0:T(8,128)(2,1)S(1)} %copy-done, bf16[64,128,128]{2,1,0:T(8,128)(2,1)} %gather_fusion.7, pred[64]{0:T(512)(128)(4,1)S(1)} %copy-done.8), kind=kOutput, calls=%fused_computation.19 | convolution fusion | flops 269484032 | bytes 8388672 | tf_op jit(solution)/shard_map/nkc,kbc->nkb/dot_general | solution.py:99
  216.9 72.2 %all-gather.6.cloned.1.call-done = bf16[128,16384]{0,1:T(8,128)(2,1)} async-done(((bf16[128,512]{0,1:T(8,128)(2,1)}), bf16[128,16384]{0,1:T(8,128)(2,1)}) %all-gather.6.cloned.1.call-update) | async-done | bytes 4194320 | tf_op jit(solution)/shard_map/all_gather | solution.py:71
  289.1 6.5 %copy.119 = bf16[128,128,128]{2,0,1:T(8,128)(2,1)} copy(bf16[128,128,128]{0,2,1:T(8,128)(2,1)} %bitcast.111) | data formatting | bytes 8388608 | tf_op jit(solution)/shard_map/reshape | solution.py:28
  295.6 2.8 gather_fusion.3
  298.5 2.1 gather_fusion.4
  300.6 4.6 %convert_bitcast_fusion = bf16[1,64,128,128]{3,2,1,0:T(8,128)(2,1)} fusion(bf16[64,128,128]{2,1,0:T(8,128)(2,1)} %gather_fusion.4, pred[64]{0:T(512)(128)(4,1)S(1)} %get-tuple-element.32, bf16[64,128,128]{2,1,0:T(8,128)(2,1)} %gather_fusion.5, pred[64]{0:T(512)(128)(4,1)S(1)} %get-tuple-element.19), kind=kOutput, calls=%fused_computation.37 | convolution fusion | flops 271581184 | bytes 6291584 | tf_op jit(solution)/shard_map/nkb,nkc->kbc/dot_general | solution.py:80
  305.8 6.1 %fusion.36 = bf16[128,32,128]{2,1,0:T(8,128)(2,1)S(1)} fusion(f32[128,64,128]{2,0,1:T(8,128)} %convolution_bitcast_fusion, s32[64]{0:T(128)S(1)} %copy-done.16), kind=kOutput, calls=%fused_computation.45 | convolution fusion | flops 403179520 | bytes 5243136 | tf_op jit(solution)/shard_map/nkb,kr->nrb/dot_general | solution.py:100
  312.4 2.8 copy.130
  315.7 22.4 %reduce.15 = bf16[4096,128]{1,0:T(8,128)(2,1)S(1)} reduce(bf16[4096,1,128]{2,1,0:T(2,128)(2,1)S(1)} %bitcast.106, bf16[]{:T(256)} %broadcast.486), dimensions={1}, to_apply=%bitcast.95.reduce_sub_computation | reduce | bytes 2097154
  339.2 7.0 %all-to-all-start.2 = ((bf16[32,2,8192]{2,1,0:T(2,128)(2,1)}), bf16[32,2,8192]{2,1,0:T(2,128)(2,1)S(1)}, u32[]{:S(2)}, u32[]{:S(2)}) async-start(bf16[32,2,8192]{2,1,0:T(2,128)(2,1)} %reshape.361), calls=%async_computation.2 | async-start | bytes 2097152 | tf_op jit(solution)/shard_map/all_to_all | solution.py:107
  346.3 2.4 convolution_bitcast_fusion.2
  348.7 4.1 fusion.39
  354.0 5.0 %copy.123 = bf16[1,128,4096]{1,0,2:T(2,128)(2,1)S(1)} copy(bf16[1,128,4096]{2,1,0:T(8,128)(2,1)} %reshape.230) | data formatting | bytes 2097152 | tf_op jit(solution)/shard_map/reshape | solution.py:78
  359.1 23.4 %reduce.14 = bf16[4096,128]{1,0:T(8,128)(2,1)} reduce(bf16[4096,1,128]{2,1,0:T(2,128)(2,1)S(1)} %bitcast.107, bf16[]{:T(256)} %broadcast.486), dimensions={1}, to_apply=%bitcast.93.reduce_sub_computation | reduce | bytes 2097154
  382.4 2.2 reshape.359
  384.6 9.8 %all-to-all-start = ((bf16[32,2,8192]{2,1,0:T(2,128)(2,1)}), bf16[32,2,8192]{2,1,0:T(2,128)(2,1)}, u32[]{:S(2)}, u32[]{:S(2)}) async-start(bf16[32,2,8192]{2,1,0:T(2,128)(2,1)} %reshape.359), calls=%async_computation | async-start | bytes 2097152 | tf_op jit(solution)/shard_map/all_to_all | solution.py:106
  397.2 22.0 %all-to-all-done = bf16[32,2,8192]{2,1,0:T(2,128)(2,1)} async-done(((bf16[32,2,8192]{2,1,0:T(2,128)(2,1)}), bf16[32,2,8192]{2,1,0:T(2,128)(2,1)}, u32[]{:S(2)}, u32[]{:S(2)}) %all-to-all-start) | async-done | bytes 1048608 | tf_op jit(solution)/shard_map/all_to_all | solution.py:106
  419.2 5.8 %reshape.360 = bf16[4096,1,128]{2,1,0:T(2,128)(2,1)} reshape(bf16[32,2,8192]{2,1,0:T(2,128)(2,1)} %all-to-all-done) | data formatting | bytes 2097152
  (118 shorter events, 27.1 us)
Async XLA Ops:
  7.2 95.7 %copy-start = (bf16[1,64,128,128]{3,2,1,0:T(8,128)(2,1)S(1)}, bf16[1,64,128,128]{3,2,1,0:T(8,128)(2,1)}, u32[]{:S(2)}) copy-start(bf16[1,64,128,128]{3,2,1,0:T(8,128)(2,1)} %param.16) | copy-start | bytes 6291460
  7.2 17.2 %copy-start.5 = (s32[128]{0:T(128)S(1)}, s32[128]{0:T(128)}, u32[]{:S(2)}) copy-start(s32[128]{0:T(128)} %param.20) | copy-start | bytes 1540
  7.2 19.1 %copy-start.4 = (s32[128,32]{0,1:T(8,128)S(1)}, s32[128,32]{0,1:T(8,128)}, u32[]{:S(2)}) copy-start(s32[128,32]{0,1:T(8,128)} %param.19) | copy-start | bytes 49156
  7.2 91.9 %all-gather.4.cloned.1.call-start = ((), (), s32[]{:S(2)}) async-start(), calls=%async_computation.5 | async-start | bytes 1081344 | tf_op jit(solution)/shard_map/all_gather | solution.py:45
  10.9 42.3 %all-to-all-start.1 = ((bf16[32,128,128]{2,1,0:T(8,128)(2,1)}), bf16[32,128,128]{2,1,0:T(8,128)(2,1)S(1)}, u32[]{:S(2)}, u32[]{:S(2)}) async-start(bf16[32,128,128]{2,1,0:T(8,128)(2,1)} %stack.2), calls=%async_computation.1 | async-start | bytes 2097152 | tf_op jit(solution)/shard_map/all_to_all | solution.py:47
  24.3 163.8 %all-gather.8.cloned.1.call-start = ((), (), s32[]{:S(2)}) async-start(), calls=%async_computation.7 | async-start | bytes 4325376 | tf_op jit(solution)/shard_map/all_gather | solution.py:90
  29.0 0.5 copy-start.13
  29.0 30.2 %copy-start.6 = (s32[64]{0:T(128)}, s32[64]{0:T(128)S(1)}, u32[]{:S(2)}) copy-start(s32[64]{0:T(128)S(1)} %get-tuple-element.33) | copy-start | bytes 772
  59.2 4.7 %copy-start.11 = (s32[32,4]{0,1:T(4,128)S(1)}, s32[32,4]{0,1:T(4,128)}, u32[]{:S(2)}) copy-start(s32[32,4]{0,1:T(4,128)} %param.17) | copy-start | bytes 1540
  59.2 5.0 %copy-start.3 = (bf16[128,512]{1,0:T(8,128)(2,1)S(1)}, bf16[128,512]{1,0:T(8,128)(2,1)}, u32[]{:S(2)}) copy-start(bf16[128,512]{1,0:T(8,128)(2,1)} %param.15) | copy-start | bytes 393220
  63.8 225.3 %all-gather.6.cloned.1.call-start = ((), (), s32[]{:S(2)}) async-start(), calls=%async_computation.6 | async-start | bytes 4325376 | tf_op jit(solution)/shard_map/all_gather | solution.py:71
  67.2 0.5 copy-start.15
  67.2 35.7 %copy-start.9 = (pred[64]{0:T(512)(128)(4,1)}, pred[64]{0:T(512)(128)(4,1)S(1)}, u32[]{:S(2)}) copy-start(pred[64]{0:T(512)(128)(4,1)S(1)} %get-tuple-element.38) | copy-start | bytes 196
  188.1 9.2 %copy-start.17 = (s32[64]{0:T(128)S(1)}, s32[64]{0:T(128)}, u32[]{:S(2)}) copy-start(s32[64]{0:T(128)} %get-tuple-element.14) | copy-start | bytes 772
  188.1 9.2 %copy-start.18 = (pred[4]{0:T(512)(128)(4,1)S(1)}, pred[4]{0:T(512)(128)(4,1)}, u32[]{:S(2)}) copy-start(pred[4]{0:T(512)(128)(4,1)} %get-tuple-element.15) | copy-start | bytes 16
  188.1 9.2 %copy-start.19 = (pred[4]{0:T(512)(128)(4,1)S(1)}, pred[4]{0:T(512)(128)(4,1)}, u32[]{:S(2)}) copy-start(pred[4]{0:T(512)(128)(4,1)} %get-tuple-element.17) | copy-start | bytes 16
  204.2 223.6 %reduce-scatter.3.cloned.1.call-start = ((), (), s32[]{:S(2)}) async-start(), calls=%async_computation.8 | async-start | bytes 2228224 | tf_op jit(solution)/shard_map/reduce_scatter | solution.py:112
  204.3 2.2 copy-start.8
  204.3 2.2 copy-start.10
  211.0 0.7 copy-start.12
  211.0 0.7 copy-start.7
  211.1 216.7 %reduce-scatter.5.cloned.1.call-start = ((), (), s32[]{:S(2)}) async-start(), calls=%async_computation.9 | async-start | bytes 2228224 | tf_op jit(solution)/shard_map/reduce_scatter | solution.py:115
  305.2 0.6 copy-start.16
  338.1 8.2 %copy-start.2 = (bf16[64,128,128]{2,1,0:T(8,128)(2,1)S(1)}, bf16[64,128,128]{2,1,0:T(8,128)(2,1)}, u32[]{:S(2)}) copy-start(bf16[64,128,128]{2,1,0:T(8,128)(2,1)} %gather_fusion.4) | copy-start | bytes 6291460
  339.2 45.4 %all-to-all-start.2 = ((bf16[32,2,8192]{2,1,0:T(2,128)(2,1)}), bf16[32,2,8192]{2,1,0:T(2,128)(2,1)S(1)}, u32[]{:S(2)}, u32[]{:S(2)}) async-start(bf16[32,2,8192]{2,1,0:T(2,128)(2,1)} %reshape.361), calls=%async_computation.2 | async-start | bytes 2097152 | tf_op jit(solution)/shard_map/all_to_all | solution.py:107
  346.3 2.4 copy-start.14
  384.6 34.6 %all-to-all-start = ((bf16[32,2,8192]{2,1,0:T(2,128)(2,1)}), bf16[32,2,8192]{2,1,0:T(2,128)(2,1)}, u32[]{:S(2)}, u32[]{:S(2)}) async-start(bf16[32,2,8192]{2,1,0:T(2,128)(2,1)} %reshape.359), calls=%async_computation | async-start | bytes 2097152 | tf_op jit(solution)/shard_map/all_to_all | solution.py:106
  425.0 2.8 copy-start.1
Sparse Core Ops, SparseCore 0:
  11.8 87.2 all-gather.3
  102.8 85.2 all-gather.7
  204.3 84.7 all-gather.5
  292.3 59.0 reduce-scatter.2
  354.7 61.5 reduce-scatter.4
